TPU v7x, 32 devices: a whole 2x2x4 slice. The times are simulated.
32 devices in a mesh: macro: 8 (over z, core), cell: 4 (over y, x).
Axes of the slice: x: 2, y: 2, z: 4, core: 2. Of those that a mesh axis runs over, the one named last changes fastest.
Arguments:
- coarse_thermal_field: float32 [32, 64, 128], P('macro', 'cell'), may hold values from -6 to 6
- representative_unit_choice: int32 [32, 64, 128], P('macro', 'cell'), may hold values from 0 to 7, as said below
- inspected_fine_location: int32 [3, 32, 64, 128], P(None, 'macro', 'cell'), may hold values from 0 to 63
- void_solid_labelling: int32 [8, 64, 4096], P('macro', 'cell'), may hold values from 0 to 1, as said below
- material_conductance_pairs: float32 [8, 2], P('macro'), may hold values from 0.2 to 4
Outputs:
- flux: float32 [3, 32, 64, 128], P(None, 'macro', 'cell')
- probe_flux: float32 [3, 32, 64, 128], P(None, 'macro', 'cell')
Inputs may be any that keep to these rules, and one draw needn't show every extreme that they name: Within the macro cells held by one device (4 x 16 x 128 cells, one index of macro with one index of cell), no pair of a unit cell s = representative_unit_choice and a slab inspected_fine_location[0] // 16 occurs more than 512 times, and one pair, the same for every device, occurs exactly 512 times on every device. `void_solid_labelling`: 1 marks a pore cell, 0 a solid cell.
All inputs are finite; a program needn't handle non-finite values.
Results may differ from a plain program's by a relative error of at most 0.0003.
Values sent between devices are 32-bit elements; how exact they have to be, the bound alone decides.
A program may use at most 128 MiB of HBM per device.

v0:
```python
import math

import jax
import jax.numpy as jnp
from jax import lax
from jax.sharding import PartitionSpec as P

ITERS = 2


highest = lax.Precision.HIGHEST


def with_halo(value, sides, width):
    for axis, dim in sides:
        peers, length = (lax.axis_size(axis), value.shape[dim])
        up = [(i, (i + 1) % peers) for i in range(peers - 1)]
        down = [(j, i) for i, j in up]
        last = lax.slice_in_dim(value, length - width, length, axis=dim)
        initial = lax.slice_in_dim(value, 0, width, axis=dim)
        before = lax.ppermute(last, axis, up)
        after = lax.ppermute(initial, axis, down)
        value = jnp.concatenate([before, value, after], axis=dim)
    return value


def dft_tables(length):
    grid_index = jnp.arange(length, dtype=jnp.int32)
    phases = grid_index[:, None] * grid_index[None, :] % length
    angles = phases.astype(jnp.float32) * (2.0 * math.pi / length)
    return (jnp.cos(angles), jnp.sin(angles))


def wave_numbers(grid_index, length):
    return jnp.where(grid_index < length // 2, grid_index, grid_index - length).astype(jnp.float32)


def rotate(values, length):
    return jnp.concatenate([values[..., length:], -values[..., :length]], axis=-1)


def slab_forward(fields, cosine, sines):
    length = cosine.shape[0]
    to_complex = jnp.concatenate([cosine, -sines], axis=1)
    along_z = jnp.einsum("nyxz,zk->nyxk", fields, to_complex, precision=highest)
    return jnp.einsum("ky,nyxz->nkxz", cosine, along_z, precision=highest) + jnp.einsum(
        "ky,nyxz->nkxz", sines, rotate(along_z, length), precision=highest
    )


def slab_inverse(spectra, cosine, sines):
    length = cosine.shape[0]
    along_y = jnp.einsum("yk,nkxz->nyxz", cosine, spectra, precision=highest) - jnp.einsum(
        "yk,nkxz->nyxz", sines, rotate(spectra, length), precision=highest
    )
    to_real = jnp.concatenate([cosine, -sines], axis=0)
    inverse_scale = 1.0 / (length * length * length)
    return jnp.einsum("nyxz,zk->nyxk", along_y, to_real, precision=highest) * inverse_scale


def pencil_forward(values, cosine, sines):
    length = cosine.shape[0]
    return jnp.einsum("kx,mbxz->mbkz", cosine, values, precision=highest) + jnp.einsum(
        "kx,mbxz->mbkz", sines, rotate(values, length), precision=highest
    )


def pencil_inverse(values, cosine, sines):
    length = cosine.shape[0]
    return jnp.einsum("xk,mbkz->mbxz", cosine, values, precision=highest) - jnp.einsum(
        "xk,mbkz->mbxz", sines, rotate(values, length), precision=highest
    )


def apply_tensor(coefficients, gradients):
    outputs = []
    for component in range(3):
        total = coefficients[component, 0] * gradients[0]
        total = total + coefficients[component, 1] * gradients[1]
        total = total + coefficients[component, 2] * gradients[2]
        outputs.append(-total)
    return jnp.stack(outputs)


def shards(
    coarse_thermal_field,
    representative_unit_choice,
    inspected_fine_location,
    void_solid_labelling,
    material_conductance_pairs,
):
    cell_count = lax.axis_size("cell")
    slab_depth = void_solid_labelling.shape[1]
    length = slab_depth * cell_count
    band_width = length // cell_count
    cosine, sines = dft_tables(length)
    grid_index = jnp.arange(length, dtype=jnp.int32)
    band_index = lax.axis_index("cell") * band_width + jnp.arange(band_width, dtype=jnp.int32)
    wave_y = wave_numbers(band_index, length)[:, None, None]
    wave_x = wave_numbers(grid_index, length)[None, :, None]
    wave_z = jnp.tile(wave_numbers(grid_index, length), 2)[None, None, :]
    solid_k = material_conductance_pairs[0, 0]
    pore_k = material_conductance_pairs[0, 1]
    ref_k = 0.5 * (solid_k + pore_k)
    squared = wave_x * wave_x + wave_y * wave_y + wave_z * wave_z
    factor = jnp.where(squared > 0, -1.0 / (ref_k * jnp.maximum(squared, 1.0)), 0.0)
    phase_cells = void_solid_labelling[0].reshape(slab_depth, length, length).transpose(1, 0, 2)
    local_k = jnp.where(phase_cells == 1, pore_k, solid_k)
    identity = jnp.eye(3, dtype=jnp.float32)[:, :, None, None, None]
    contrast = local_k - ref_k
    gradient = jnp.broadcast_to(identity, (3, 3, length, slab_depth, length))
    first_sweep = 0
    for sweep in range(first_sweep, ITERS):
        polar = (contrast * gradient).reshape(9, length, slab_depth, length)
        spectra = slab_forward(polar, cosine, sines).reshape(3, 3, length, slab_depth, 2 * length)
        project_received = lax.all_to_all(spectra, "cell", split_axis=2, concat_axis=3, tiled=True)
        project_item_count = project_received.shape[0]
        project_flattened = project_received.reshape(
            project_item_count * 3, band_width, length, 2 * length
        )
        project_spectra = pencil_forward(project_flattened, cosine, sines).reshape(
            project_item_count, 3, band_width, length, 2 * length
        )
        projected = (
            wave_x * project_spectra[:, 0]
            + wave_y * project_spectra[:, 1]
            + wave_z * project_spectra[:, 2]
        )
        project_response = jnp.stack(
            [wave_x * projected * factor, wave_y * projected * factor, wave_z * projected * factor],
            axis=1,
        )
        item_count = project_response.shape[0]
        flattened = project_response.reshape(item_count * 3, band_width, length, 2 * length)
        spatial = pencil_inverse(flattened, cosine, sines)
        back_returned = lax.all_to_all(spatial, "cell", split_axis=2, concat_axis=1, tiled=True)
        spectral_response = back_returned.reshape(item_count, 3, length, slab_depth, 2 * length)
        update = slab_inverse(
            spectral_response.reshape(9, length, slab_depth, 2 * length), cosine, sines
        )
        gradient = identity + update.reshape(3, 3, length, slab_depth, length)
    weighted = local_k * gradient
    partial_sums = jnp.sum(weighted, axis=(2, 3, 4))
    totals = lax.psum(partial_sums, "cell")
    tensor = (totals / (length * length * length)).T
    flux_table = (-weighted).reshape(3, 3, length * slab_depth * length)
    enlarged_span = with_halo(coarse_thermal_field, (("macro", 0), ("cell", 1)), 1)
    grad_x = (enlarged_span[2:, 1:-1] - enlarged_span[:-2, 1:-1]) * 0.5
    grad_y = (enlarged_span[1:-1, 2:] - enlarged_span[1:-1, :-2]) * 0.5
    enlarged_third_span = jnp.pad(coarse_thermal_field, ((0, 0), (0, 0), (1, 1)))
    grad_z = (enlarged_third_span[:, :, 2:] - enlarged_third_span[:, :, :-2]) * 0.5
    block_spans_list = coarse_thermal_field.shape
    row_count = block_spans_list[0] * block_spans_list[1] * block_spans_list[2]
    gradients = jnp.stack([grad_x, grad_y, grad_z]).reshape(3, row_count)
    sample_ids = representative_unit_choice.reshape(row_count)
    probe_x = inspected_fine_location[0].reshape(row_count)
    probe_y = inspected_fine_location[1].reshape(row_count)
    probe_z = inspected_fine_location[2].reshape(row_count)
    owners = probe_x // slab_depth
    offsets = (probe_y * slab_depth + probe_x % slab_depth) * length + probe_z
    macro_count = lax.axis_size("macro")
    device_count = macro_count * cell_count
    capacity = 2 * row_count // device_count
    targets = sample_ids * cell_count + owners
    ordering = jnp.argsort(targets, stable=True)
    sorted_targets = targets[ordering]
    starts = jnp.searchsorted(
        sorted_targets, jnp.arange(device_count, dtype=jnp.int32), side="left"
    )
    position = jnp.arange(row_count, dtype=jnp.int32) - starts[sorted_targets]
    slot_index = sorted_targets * capacity + position
    payload = jnp.concatenate([gradients, offsets.astype(jnp.float32)[None]], axis=0)[:, ordering]
    outgoing = jnp.zeros((4, device_count * capacity), jnp.float32).at[:, slot_index].set(payload)
    received = lax.all_to_all(
        lax.all_to_all(
            outgoing.reshape(4, macro_count, cell_count, capacity),
            "macro",
            split_axis=1,
            concat_axis=1,
            tiled=True,
        ),
        "cell",
        split_axis=2,
        concat_axis=2,
        tiled=True,
    )
    slot_count = device_count * capacity
    got_grad = received[:3].reshape(3, slot_count)
    got_offset = received[3].reshape(slot_count).astype(jnp.int32)
    probe_rows = []
    for component in range(3):
        total = flux_table[0, component][got_offset] * got_grad[0]
        total = total + flux_table[1, component][got_offset] * got_grad[1]
        total = total + flux_table[2, component][got_offset] * got_grad[2]
        probe_rows.append(total)
    probe_values = jnp.stack(probe_rows)
    answers = jnp.concatenate([apply_tensor(tensor, got_grad), probe_values], axis=0)
    returned = lax.all_to_all(
        lax.all_to_all(
            answers.reshape(6, macro_count, cell_count, capacity),
            "macro",
            split_axis=1,
            concat_axis=1,
            tiled=True,
        ),
        "cell",
        split_axis=2,
        concat_axis=2,
        tiled=True,
    )
    back_sorted = returned.reshape(6, slot_count)[:, slot_index]
    both_rows = jnp.zeros((6, row_count), jnp.float32).at[:, ordering].set(back_sorted)
    flux_rows = both_rows[:3]
    probe_out = both_rows[3:]
    return (flux_rows.reshape((3,) + block_spans_list), probe_out.reshape((3,) + block_spans_list))


def solution(mesh):
    in_specs = (
        P("macro", "cell", None),
        P("macro", "cell", None),
        P(None, "macro", "cell", None),
        P("macro", "cell", None),
        P("macro", None),
    )
    out_specs = (P(None, "macro", "cell", None), P(None, "macro", "cell", None))
    return jax.shard_map(shards, mesh=mesh, in_specs=in_specs, out_specs=out_specs, check_vma=False)
```

profile of v0, /device:TPU:0, one launch (start us, length us, event | category | flops | bytes accessed | tf_op | source)
XLA Modules:
  0.0 1510.6 jit_solution(2688933325964675870)
XLA Ops:
  7.1 4.1 fusion.44
  14.3 6.3 fusion.36
  20.5 5.8 fusion.56
  26.3 4.8 copy.75
  31.2 5.3 all-to-all-start
  40.3 6.8 sort.17
  47.7 45.5 %gather_fusion.1 = s32[8192]{0:T(1024)S(1)} fusion(s32[8192]{0:T(1024)S(1)} %fusion.88, s32[8192]{0:T(1024)S(1)} %get-tuple-element.181), kind=kCustom, calls=%fused_computation.1 | custom fusion | bytes 98304 | tf_op jit(solution)/shard_map/gather | solution.py:166
  93.2 10.5 while.24
  105.3 4.5 compare_select_fusion.6
  112.6 15.6 %select_select_fusion = s32[8192]{0:T(1024)S(1)} fusion(pred[8192]{0:T(1024)(128)(4,1)S(1)} %get-tuple-element.119, pred[8192]{0:T(1024)(128)(4,1)S(1)} %get-tuple-element.118, pred[8192]{0:T(1024)(128)(4,1)S(1)} %get-tuple-element.117, pred[8192]{0:T(1024)(128)(4,1)S(1)} %get-tuple-element.116, pred[8192]{0:T(1024)(128)(4,1)S(1)} %get-tuple-element.115, ...), kind=kLoop, calls=%fused_computation.220 | loop fusion | flops 204800 | bytes 270436 | tf_op jit(solution)/shard_map/gather | solution.py:170
  130.0 4.8 collective-permute-start.3
  138.9 70.3 %scatter_custom_fusion = f32[4,16384]{0,1:T(8,128)} fusion(s32[8192]{0:T(1024)S(1)} %bitcast.209, f32[4,8192]{0,1:T(8,128)} %copy.97, s32[8192]{0:T(1024)S(1)} %get-tuple-element.181, f32[]{:T(128)} %constant.96.clone.1), kind=kCustom, calls=%fused_computation.84 | custom fusion | bytes 262656 | tf_op jit(solution)/shard_map/scatter | solution.py:173
  209.2 5.9 copy.98
  215.1 8.3 all-to-all-start.4
  223.4 3.1 copy.76
  228.7 4.9 fusion.110
  233.6 5.5 fusion.75
  243.1 4.9 fusion.108
  248.0 5.9 subtract_bitcast_fusion.3
  254.0 4.9 copy.77
  258.8 5.7 all-to-all-start.1
  265.4 54.3 %all-to-all-done.1 = f32[9,16,64,128]{3,1,0,2:T(8,128)} async-done(((f32[9,16,64,128]{3,1,0,2:T(8,128)}), f32[9,16,64,128]{3,1,0,2:T(8,128)}, u32[]{:S(2)}, u32[]{:S(2)}) %all-to-all-start.1) | async-done | bytes 4718624 | tf_op jit(solution)/shard_map/all_to_all | solution.py:136
  319.7 3.4 all-to-all-start.5
  323.2 4.3 copy.79
  328.9 6.1 fusion.106
  337.2 5.7 subtract_bitcast_fusion.2
  342.9 6.4 fusion.34
  349.4 4.5 fusion.40
  357.0 5.8 fusion.30
  362.8 6.2 fusion.59
  368.9 4.9 copy.87
  374.5 5.2 all-to-all-start.2
  381.9 51.3 %all-to-all-done.2 = f32[3,3,64,16,128]{4,3,1,0,2:T(8,128)} async-done(((f32[3,3,64,16,128]{4,3,1,0,2:T(8,128)}), f32[3,3,64,16,128]{4,3,1,0,2:T(8,128)}, u32[]{:S(2)}, u32[]{:S(2)}) %all-to-all-start.2) | async-done | bytes 4718624 | tf_op jit(solution)/shard_map/all_to_all | solution.py:116
  433.3 3.0 copy.88
  438.5 4.9 fusion.103
  443.4 5.9 fusion.68
  453.9 4.9 fusion.101
  458.8 5.7 subtract_bitcast_fusion.1
  464.5 4.9 copy.89
  469.4 4.9 all-to-all-start.3
  474.4 52.8 %all-to-all-done.3 = f32[9,16,64,128]{3,1,0,2:T(8,128)} async-done(((f32[9,16,64,128]{3,1,0,2:T(8,128)}), f32[9,16,64,128]{3,1,0,2:T(8,128)}, u32[]{:S(2)}, u32[]{:S(2)}) %all-to-all-start.3) | async-done | bytes 4718624 | tf_op jit(solution)/shard_map/all_to_all | solution.py:136
  527.2 4.3 copy.91
  533.0 6.1 fusion.99
  541.3 5.9 subtract_bitcast_fusion
  547.3 8.0 multiply_reduce_fusion
  555.2 4.2 reshape.386
  562.0 90.5 %gather_fusion.8 = f32[16384]{0:T(1024)S(1)} fusion(f32[65536]{0:T(1024)S(1)} %bitcast.179, s32[16384]{0:T(1024)S(1)} %broadcast_clamp_fusion), kind=kCustom, calls=%fused_computation.9 | custom fusion | bytes 196608 | tf_op jit(solution)/shard_map/gather | solution.py:192
  653.2 90.5 %gather_fusion.9 = f32[16384]{0:T(1024)S(1)} fusion(f32[65536]{0:T(1024)S(1)} %bitcast.178, s32[16384]{0:T(1024)S(1)} %broadcast_clamp_fusion), kind=kCustom, calls=%fused_computation.10 | custom fusion | bytes 196608 | tf_op jit(solution)/shard_map/gather | solution.py:193
  743.8 90.5 %gather_fusion.10 = f32[16384]{0:T(1024)S(1)} fusion(f32[65536]{0:T(1024)S(1)} %bitcast.177, s32[16384]{0:T(1024)S(1)} %broadcast_clamp_fusion), kind=kCustom, calls=%fused_computation.11 | custom fusion | bytes 196608 | tf_op jit(solution)/shard_map/gather | solution.py:194
  834.4 90.5 %gather_fusion.5 = f32[16384]{0:T(1024)S(1)} fusion(f32[65536]{0:T(1024)S(1)} %bitcast.176, s32[16384]{0:T(1024)S(1)} %broadcast_clamp_fusion), kind=kCustom, calls=%fused_computation.6 | custom fusion | bytes 196608 | tf_op jit(solution)/shard_map/gather | solution.py:192
  924.9 90.5 %gather_fusion.6 = f32[16384]{0:T(1024)S(1)} fusion(f32[65536]{0:T(1024)S(1)} %bitcast.175, s32[16384]{0:T(1024)S(1)} %broadcast_clamp_fusion), kind=kCustom, calls=%fused_computation.7 | custom fusion | bytes 196608 | tf_op jit(solution)/shard_map/gather | solution.py:193
  1015.5 90.7 %gather_fusion.7 = f32[16384]{0:T(1024)S(1)} fusion(f32[65536]{0:T(1024)S(1)} %bitcast.174, s32[16384]{0:T(1024)S(1)} %broadcast_clamp_fusion), kind=kCustom, calls=%fused_computation.8 | custom fusion | bytes 196608 | tf_op jit(solution)/shard_map/gather | solution.py:194
  1106.3 90.5 %gather_fusion.2 = f32[16384]{0:T(1024)S(1)} fusion(f32[65536]{0:T(1024)S(1)} %bitcast.173, s32[16384]{0:T(1024)S(1)} %broadcast_clamp_fusion), kind=kCustom, calls=%fused_computation.3 | custom fusion | bytes 196608 | tf_op jit(solution)/shard_map/gather | solution.py:192
  1196.8 90.5 %gather_fusion.3 = f32[16384]{0:T(1024)S(1)} fusion(f32[65536]{0:T(1024)S(1)} %bitcast.172, s32[16384]{0:T(1024)S(1)} %broadcast_clamp_fusion), kind=kCustom, calls=%fused_computation.4 | custom fusion | bytes 196608 | tf_op jit(solution)/shard_map/gather | solution.py:193
  1287.5 90.5 %gather_fusion.4 = f32[16384]{0:T(1024)S(1)} fusion(f32[65536]{0:T(1024)S(1)} %bitcast.171, s32[16384]{0:T(1024)S(1)} %broadcast_clamp_fusion), kind=kCustom, calls=%fused_computation.5 | custom fusion | bytes 196608 | tf_op jit(solution)/shard_map/gather | solution.py:194
  1378.1 8.9 psum.7
  1394.4 16.6 %all_to_all.86 = f32[6,8,4,512]{3,2,0,1:T(4,128)S(1)} all-to-all(f32[6,8,4,512]{3,2,0,1:T(4,128)S(1)} %copy.104), channel_id=1, replica_groups=mesh['macro'=8,'cell'=4] {'macro'}, dimensions={1} | all-to-all | bytes 786432 | tf_op jit(solution)/shard_map/all_to_all | solution.py:199
  1411.9 3.5 all-to-all-start.7
  1415.4 6.6 all-to-all-done.7
  1422.1 4.6 copy.106
  1426.7 68.9 %scatter_custom_fusion.1 = f32[6,8192]{0,1:T(8,128)} fusion(s32[8192]{0:T(1024)} %get-tuple-element.182, f32[6,16384]{0,1:T(8,128)} %bitcast.201, s32[8192]{0:T(1024)S(1)} %broadcast_clamp_fusion.1, f32[]{:T(128)} %constant.96.clone.1), kind=kCustom, calls=%fused_computation.82 | custom fusion | bytes 197120 | tf_op jit(solution)/shard_map/scatter | solution.py:212
  1495.6 7.9 fusion.236
  1503.4 3.5 copy.107
  1506.9 3.5 copy.108
  (198 shorter events, 71.4 us)
Async XLA Ops:
  0.8 348.6 %copy-start.12 = (f32[64,64]{1,0:T(8,128)}, f32[64,64]{1,0:T(8,128)S(1)}, u32[]{:S(2)}) copy-start(f32[64,64]{1,0:T(8,128)S(1)} %get-tuple-element.229) | copy-start | bytes 49156
  0.8 12.2 copy-start.20
  5.9 7.1 copy-start.2
  6.3 0.8 copy-start.4
  31.2 5.3 copy-start.18
  31.2 9.1 copy-start.17
  31.2 9.1 copy-start.19
  31.2 183.9 %all-to-all-start = ((f32[3,3,64,16,128]{4,3,1,0,2:T(8,128)}), f32[3,3,64,16,128]{4,3,1,0,2:T(8,128)}, u32[]{:S(2)}, u32[]{:S(2)}) async-start(f32[3,3,64,16,128]{4,3,1,0,2:T(8,128)} %copy.75), calls=%async_computation | async-start | bytes 9437184 | tf_op jit(solution)/shard_map/all_to_all | solution.py:116
  36.5 92.1 %collective-permute-start.1 = (f32[1,16,128]{2,1,0:T(8,128)S(1)}, f32[1,16,128]{2,1,0:T(8,128)S(1)}, u32[]{:S(2)}, u32[]{:S(2)}) collective-permute-start(f32[1,16,128]{2,1,0:T(8,128)S(1)} %get-tuple-element.180), channel_id=1, source_target_pairs={{0,4},{4,8},{8,12},{12,16},{16,20},{20,24},{24,28},{1,5},{5,9},{9,... | collective-permute-start | bytes 24584 | tf_op jit(solution)/shard_map/ppermute | solution.py:21
  38.7 89.8 %collective-permute-start = (f32[1,16,128]{2,1,0:T(8,128)S(1)}, f32[1,16,128]{2,1,0:T(8,128)S(1)}, u32[]{:S(2)}, u32[]{:S(2)}) collective-permute-start(f32[1,16,128]{2,1,0:T(8,128)S(1)} %get-tuple-element.179), channel_id=1, source_target_pairs={{4,0},{8,4},{12,8},{16,12},{20,16},{24,20},{28,24},{5,1},{9,5},{13... | collective-permute-start | bytes 24584 | tf_op jit(solution)/shard_map/ppermute | solution.py:22
  128.3 80.9 %copy-start.15 = (s32[8192,1]{0,1:T(1,128)}, s32[8192,1]{0,1:T(1,128)S(1)}, u32[]{:S(2)}) copy-start(s32[8192,1]{0,1:T(1,128)S(1)} %compare_select_fusion.2) | copy-start | bytes 98308
  128.5 111.4 %copy-start = (f32[16,64,128]{2,1,0:T(8,128)}, f32[16,64,128]{2,1,0:T(8,128)S(1)}, u32[]{:S(2)}) copy-start(f32[16,64,128]{2,1,0:T(8,128)S(1)} %fusion.85) | copy-start | bytes 1572868
  128.7 6.1 collective-permute-start.2
  130.0 6.1 collective-permute-start.3
  215.1 43.7 %all-to-all-start.4 = ((f32[4,8,4,512]{3,2,0,1:T(4,128)}), f32[4,8,4,512]{3,2,0,1:T(4,128)S(1)}, u32[]{:S(2)}, u32[]{:S(2)}) async-start(f32[4,8,4,512]{3,2,0,1:T(4,128)} %copy.98), calls=%async_computation.4 | async-start | bytes 524288 | tf_op jit(solution)/shard_map/all_to_all | solution.py:175
  258.8 60.9 %all-to-all-start.1 = ((f32[9,16,64,128]{3,1,0,2:T(8,128)}), f32[9,16,64,128]{3,1,0,2:T(8,128)}, u32[]{:S(2)}, u32[]{:S(2)}) async-start(f32[9,16,64,128]{3,1,0,2:T(8,128)} %copy.77), calls=%async_computation.1 | async-start | bytes 9437184 | tf_op jit(solution)/shard_map/all_to_all | solution.py:136
  319.7 54.1 %all-to-all-start.5 = ((f32[4,8,4,512]{3,1,0,2:T(8,128)}), f32[4,8,4,512]{3,1,0,2:T(8,128)S(1)}, u32[]{:S(2)}, u32[]{:S(2)}) async-start(f32[4,8,4,512]{3,1,0,2:T(8,128)} %copy.99), calls=%async_computation.5 | async-start | bytes 524288 | tf_op jit(solution)/shard_map/all_to_all | solution.py:174
  342.9 6.5 copy-start.5
  373.8 5.9 copy-start.3
  373.8 0.7 copy-start.11
  374.5 58.8 %all-to-all-start.2 = ((f32[3,3,64,16,128]{4,3,1,0,2:T(8,128)}), f32[3,3,64,16,128]{4,3,1,0,2:T(8,128)}, u32[]{:S(2)}, u32[]{:S(2)}) async-start(f32[3,3,64,16,128]{4,3,1,0,2:T(8,128)} %copy.87), calls=%async_computation.2 | async-start | bytes 9437184 | tf_op jit(solution)/shard_map/all_to_all | solution.py:116
  380.0 56.3 %copy-start.6 = (f32[16,64,64]{2,0,1:T(8,128)}, f32[16,64,64]{2,0,1:T(8,128)S(1)}, u32[]{:S(2)}) copy-start(f32[16,64,64]{2,0,1:T(8,128)S(1)} %copy.166) | copy-start | bytes 786436
  443.4 6.0 copy-start.1
  469.4 57.8 %all-to-all-start.3 = ((f32[9,16,64,128]{3,1,0,2:T(8,128)}), f32[9,16,64,128]{3,1,0,2:T(8,128)}, u32[]{:S(2)}, u32[]{:S(2)}) async-start(f32[9,16,64,128]{3,1,0,2:T(8,128)} %copy.89), calls=%async_computation.3 | async-start | bytes 9437184 | tf_op jit(solution)/shard_map/all_to_all | solution.py:136
  541.3 6.0 copy-start.7
  541.3 6.0 copy-start.13
  555.2 4.3 copy-start.21
  1287.4 90.6 %copy-start.22 = (f32[9]{0:T(128)S(1)}, f32[9]{0:T(128)}, u32[]{:S(2)}) copy-start(f32[9]{0:T(128)} %get-tuple-element.226) | copy-start | bytes 112
  1287.4 100.3 %copy-start.8 = (f32[1,8,4,512]{3,1,0,2:T(8,128)S(1)}, f32[1,8,4,512]{3,1,0,2:T(8,128)}, u32[]{:S(2)}) copy-start(f32[1,8,4,512]{3,1,0,2:T(8,128)} %get-tuple-element.168) | copy-start | bytes 196612
  1287.4 100.3 %copy-start.9 = (f32[1,8,4,512]{3,1,0,2:T(8,128)S(1)}, f32[1,8,4,512]{3,1,0,2:T(8,128)}, u32[]{:S(2)}) copy-start(f32[1,8,4,512]{3,1,0,2:T(8,128)} %get-tuple-element.169) | copy-start | bytes 196612
  1287.4 100.3 %copy-start.10 = (f32[1,8,4,512]{3,1,0,2:T(8,128)S(1)}, f32[1,8,4,512]{3,1,0,2:T(8,128)}, u32[]{:S(2)}) copy-start(f32[1,8,4,512]{3,1,0,2:T(8,128)} %get-tuple-element.170) | copy-start | bytes 196612
  1287.5 106.7 %copy-start.14 = (f32[1,8,4,512]{3,2,1,0:T(4,128)S(1)}, f32[1,8,4,512]{3,2,1,0:T(4,128)}, u32[]{:S(2)}) copy-start(f32[1,8,4,512]{3,2,1,0:T(4,128)} %gather.85) | copy-start | bytes 196612
  1378.0 37.4 %copy-start.16 = (s32[8192,1]{0,1:T(1,128)S(1)}, s32[8192,1]{0,1:T(1,128)}, u32[]{:S(2)}) copy-start(s32[8192,1]{0,1:T(1,128)} %copy-done.15) | copy-start | bytes 98308
  1411.9 10.1 all-to-all-start.7
where the time goes:
time: 1520 us; the launch traced here: 1510 us
  local copies, waits for them, and re-layouts  1090 us (72%)
  waiting for transfers between devices  166 us (11%)
  matrix products  114 us (8%)
  other arithmetic  66.2 us (4%)
  starting transfers between devices  46.1 us (3%)
  blocking collectives  25.4 us (2%)
    gather x6, local copies, waits for them, and re-layouts, shards(): total = flux_table[0, component][got_offset] * got_grad[0]  272 us
    gather x6, local copies, waits for them, and re-layouts, shards(): total = total + flux_table[2, component][got_offset] * got_grad[2]  272 us
    gather x6, local copies, waits for them, and re-layouts, shards(): total = total + flux_table[1, component][got_offset] * got_grad[1]  272 us
    all_to_all x2, waiting for transfers between devices, shards(): lax.all_to_all(spatial, 'cell', split_axis=2, concat_axis=1, tiled=True)  107 us
    scatter x1, local copies, waits for them, and re-layouts, shards(): jnp.zeros((4, device_count * capacity), jnp.float32).at[:, slot_index]  70.3 us
    scatter x1, local copies, waits for them, and re-layouts, shards(): jnp.zeros((6, row_count), jnp.float32).at[:, ordering].set(back_sorted)  68.9 us
    all_to_all x2, waiting for transfers between devices, shards(): lax.all_to_all(spectra, 'cell', split_axis=2, concat_axis=3, tiled=True)  51.3 us
    gather x1, local copies, waits for them, and re-layouts, shards(): sorted_targets = targets[ordering]  45.5 us
  transfers between devices with their start and end apart: 11, of which 5 were waited for; matrix products, arithmetic and copies ran while one was open for 17% of the time, Pallas kernels for 0%

commit v1 on v0

v1 whole, which is shorter than its diff:
```python
import functools
import math

import jax
import jax.numpy as jnp
from jax import lax
from jax.experimental import pallas as pl
from jax.experimental.pallas import tpu as pltpu
from jax.sharding import PartitionSpec as P

high = lax.Precision.HIGH
highest = lax.Precision.HIGHEST
BOTH = ("macro", "cell")


def einsum(eq, a, b):
    return jnp.einsum(eq, a, b, precision=high)


def neighbours(value, axis, dim):
    peers, length = lax.axis_size(axis), value.shape[dim]
    up = [(i, i + 1) for i in range(peers - 1)]
    down = [(i + 1, i) for i in range(peers - 1)]
    before = lax.ppermute(lax.slice_in_dim(value, length - 1, length, axis=dim), axis, up)
    after = lax.ppermute(lax.slice_in_dim(value, 0, 1, axis=dim), axis, down)
    return jnp.concatenate([before, value, after], axis=dim)


def dft_tables(length):
    grid_index = jnp.arange(length, dtype=jnp.int32)
    phases = grid_index[:, None] * grid_index[None, :] % length
    angles = phases.astype(jnp.float32) * (2.0 * math.pi / length)
    return jnp.cos(angles), jnp.sin(angles)


def wave_numbers(grid_index, length):
    return jnp.where(grid_index < length // 2, grid_index, grid_index - length).astype(jnp.float32)


def rotate(values):
    half = values.shape[-1] // 2
    return jnp.concatenate([values[..., half:], -values[..., :half]], axis=-1)


def forward(eq, cosine, sines, values):
    return einsum(eq, cosine, values) + einsum(eq, sines, rotate(values))


def inverse(eq, cosine, sines, values):
    return einsum(eq, cosine, values) - einsum(eq, sines, rotate(values))


def lookup_kernel(fields, k_ref, l_ref, table_ref, out_ref, split):
    rows, depth = table_ref.shape
    length = rows // fields
    block = k_ref.shape[1]

    @pl.when(pl.program_id(0) == 0)
    def _():
        whole = table_ref[...]
        upper = whole.astype(jnp.bfloat16)
        split[:rows] = upper
        split[rows:] = (whole - upper.astype(jnp.float32)).astype(jnp.bfloat16)

    at_k = lax.broadcasted_iota(jnp.int32, (depth, block), 0) == k_ref[...]
    picked = jnp.dot(
        split[...],
        jnp.where(at_k, 1.0, 0.0).astype(jnp.bfloat16),
        preferred_element_type=jnp.float32,
    )
    at_l = lax.broadcasted_iota(jnp.int32, (length, block), 0) == l_ref[...]
    for field in range(fields):
        first = field * length
        both = picked[first : first + length] + picked[rows + first : rows + first + length]
        out_ref[field : field + 1] = jnp.sum(jnp.where(at_l, both, 0.0), axis=0, keepdims=True)


def lookup(table, k_index, l_index, block=512):
    fields, length, depth = table.shape
    count = k_index.shape[0]
    rows = fields * length
    return pl.pallas_call(
        functools.partial(lookup_kernel, fields),
        grid=(count // block,),
        in_specs=[
            pl.BlockSpec((1, block), lambda i: (0, i)),
            pl.BlockSpec((1, block), lambda i: (0, i)),
            pl.BlockSpec((rows, depth), lambda i: (0, 0)),
        ],
        out_specs=pl.BlockSpec((fields, block), lambda i: (0, i)),
        out_shape=jax.ShapeDtypeStruct((fields, count), jnp.float32),
        scratch_shapes=[pltpu.VMEM((2 * rows, depth), jnp.bfloat16)],
        compiler_params=pltpu.CompilerParams(vmem_limit_bytes=40 * 1024 * 1024),
        cost_estimate=pl.CostEstimate(
            flops=4 * rows * depth * count, bytes_accessed=4 * rows * depth, transcendentals=0
        ),
    )(k_index.reshape(1, count), l_index.reshape(1, count), table.reshape(rows, depth))


def probe_kernel(k_ref, l_ref, along_ref, waves_ref, local_ref, out_ref, mean_ref, split):
    fields, depth = along_ref.shape[:2]
    length, block = waves_ref.shape[0], k_ref.shape[1]
    rows = fields * length

    @pl.when(pl.program_id(0) == 0)
    def _():
        local_k = local_ref[...]
        for field in range(fields):
            update = lax.dot_general(
                waves_ref[...],
                along_ref[field],
                (((1,), (1,)), ((), ())),
                precision=highest,
                preferred_element_type=jnp.float32,
            )
            unit = 1.0 if field % 4 == 0 else 0.0
            values = local_k * (update + unit)
            total = jnp.sum(jnp.sum(values, axis=0, keepdims=True), axis=1, keepdims=True)
            mean_ref[field : field + 1] = jnp.broadcast_to(total, (1, mean_ref.shape[1]))
            upper = values.astype(jnp.bfloat16)
            first = field * length
            split[first : first + length] = upper
            split[rows + first : rows + first + length] = (
                values - upper.astype(jnp.float32)
            ).astype(jnp.bfloat16)

    at_k = lax.broadcasted_iota(jnp.int32, (depth, block), 0) == k_ref[...]
    picked = jnp.dot(
        split[...],
        jnp.where(at_k, 1.0, 0.0).astype(jnp.bfloat16),
        preferred_element_type=jnp.float32,
    )
    at_l = lax.broadcasted_iota(jnp.int32, (length, block), 0) == l_ref[...]
    for field in range(fields):
        first = field * length
        both = picked[first : first + length] + picked[rows + first : rows + first + length]
        out_ref[field : field + 1] = jnp.sum(jnp.where(at_l, both, 0.0), axis=0, keepdims=True)


def probe(along, waves, local_k, k_index, l_index, block=512):
    fields, depth, width = along.shape
    length = waves.shape[0]
    count = k_index.shape[0]
    rows, lanes = fields * length, 128
    return pl.pallas_call(
        probe_kernel,
        grid=(count // block,),
        in_specs=[
            pl.BlockSpec((1, block), lambda i: (0, i)),
            pl.BlockSpec((1, block), lambda i: (0, i)),
            pl.BlockSpec((fields, depth, width), lambda i: (0, 0, 0)),
            pl.BlockSpec((length, width), lambda i: (0, 0)),
            pl.BlockSpec((length, depth), lambda i: (0, 0)),
        ],
        out_specs=[
            pl.BlockSpec((fields, block), lambda i: (0, i)),
            pl.BlockSpec((fields, lanes), lambda i: (0, 0)),
        ],
        out_shape=[
            jax.ShapeDtypeStruct((fields, count), jnp.float32),
            jax.ShapeDtypeStruct((fields, lanes), jnp.float32),
        ],
        scratch_shapes=[pltpu.VMEM((2 * rows, depth), jnp.bfloat16)],
        compiler_params=pltpu.CompilerParams(vmem_limit_bytes=40 * 1024 * 1024),
        cost_estimate=pl.CostEstimate(
            flops=4 * rows * depth * count, bytes_accessed=8 * rows * depth, transcendentals=0
        ),
    )(k_index.reshape(1, count), l_index.reshape(1, count), along, waves, local_k)


def upper_lower(values):
    upper = lax.reduce_precision(values, 8, 7)
    return upper.astype(jnp.bfloat16), (values - upper).astype(jnp.bfloat16)


def one_hot(index, count):
    return (jnp.arange(count, dtype=jnp.int32)[:, None] == index[None, :]).astype(jnp.bfloat16)


def exact_dot(eq, a, b):
    return jnp.einsum(eq, a, b, preferred_element_type=jnp.float32)


def slots_of(targets, buckets, capacity):
    count = targets.shape[0]
    lanes = 128
    marks = one_hot(targets, buckets).reshape(buckets, count // lanes, lanes)
    lane = jnp.arange(lanes)
    within = exact_dot("bij,jk->bik", marks, (lane[:, None] < lane[None, :]).astype(jnp.bfloat16))
    totals = jnp.sum(marks.astype(jnp.float32), axis=2).astype(jnp.bfloat16)
    step = jnp.arange(count // lanes)
    before = exact_dot("bi,ik->bk", totals, (step[:, None] < step[None, :]).astype(jnp.bfloat16))
    rank = jnp.sum(marks * (within + before[:, :, None]), axis=0)
    return targets * capacity + rank.reshape(count).astype(jnp.int32)


def unit_fields(labels, pair, received):
    cell_count = lax.axis_size("cell")
    here = lax.axis_index("cell")
    slab = labels.shape[1]
    length = slab * cell_count
    cosine, sines = dft_tables(length)
    grid_index = jnp.arange(length, dtype=jnp.int32)
    waves = wave_numbers(grid_index, length)
    wave_z = jnp.tile(waves, 2)
    wx, wy, wz = waves[:, None, None], waves[None, :, None], wave_z[None, None, :]
    solid_k, pore_k = pair[0, 0], pair[0, 1]
    ref_k = 0.5 * (solid_k + pore_k)
    half = 0.5 * (pore_k - solid_k)
    to_complex = jnp.concatenate([cosine, -sines], axis=1)
    to_real = jnp.concatenate([cosine, -sines], axis=0) * (1.0 / (length * length * length))

    def factor_of(squared):
        return jnp.where(squared > 0, -1.0 / (ref_k * jnp.maximum(squared, 1.0)), 0.0)

    whole = lax.all_gather(labels[0], "cell", axis=0, tiled=True)
    sign = jnp.where(whole == 1, 1.0, -1.0).reshape(length, length, length)
    own = jnp.where(labels[0] == 1, 1.0, -1.0).reshape(slab, length, length)

    spectrum = einsum("xyz,zk->xyk", sign, to_complex)
    spectrum = forward("ky,xyz->xkz", cosine, sines, spectrum)
    spectrum = forward("kx,xyz->kyz", cosine, sines, spectrum)
    base = spectrum * (factor_of(wx * wx + wy * wy + wz * wz) * half)
    powers = jnp.stack([wx * wx * base, wx * base, base])
    slab_cos = lax.dynamic_slice_in_dim(cosine, here * slab, slab, axis=0)
    slab_sin = lax.dynamic_slice_in_dim(sines, here * slab, slab, axis=0)
    two, one, zero = inverse("xk,mkyz->mxyz", slab_cos, slab_sin, powers)
    wk = waves[None, :, None]
    by_y = inverse(
        "yk,mxkz->mxyz",
        cosine,
        sines,
        jnp.stack([two, wk * one, one, wk * wk * zero, wk * zero, zero]),
    )
    ones = jnp.ones_like(wave_z)
    z_scale = jnp.stack([ones, ones, wave_z, ones, wave_z, wave_z * wave_z])
    update = einsum("mxyk,kz->mxyz", by_y * z_scale[:, None, None, :], to_real)
    unit = jnp.array([1.0, 0.0, 0.0, 1.0, 0.0, 1.0], jnp.float32)[:, None, None, None]
    polar = (own * half) * (update + unit)

    along = einsum("mxyz,zk->mxyk", polar, to_complex)
    xx, xy, xz, yy, yz, zz = forward("ky,mxyz->mkxz", cosine, sines, along)
    wk = waves[:, None, None]
    sent = jnp.stack([xx, xy, xz, wk * xy + wz * xz, wk * yy + wz * yz, wk * yz + wz * zz])
    sent, received = lax.optimization_barrier((sent, received))
    band = lax.all_to_all(sent, "cell", split_axis=1, concat_axis=2, tiled=True)
    band = forward("kx,mbxz->mbkz", cosine, sines, band)
    band_y = wave_numbers(here * slab + jnp.arange(slab, dtype=jnp.int32), length)[:, None, None]
    band_x = waves[None, :, None]
    projected = (band_x * band[:3] + band[3:]) * factor_of(
        band_x * band_x + band_y * band_y + wz * wz
    )
    back = inverse("xk,mbkz->mbxz", cosine, sines, jnp.concatenate([band_x * projected, projected]))
    back = lax.all_to_all(back, "cell", split_axis=2, concat_axis=1, tiled=True)
    rx, r1 = back[:3], back[3:]
    parts = jnp.stack([rx, wk * r1, wz * r1], axis=1).reshape(9, length, slab, 2 * length)
    along = inverse("yk,nkxz->nxyz", cosine, sines, parts)
    local_k = jnp.where(labels[0] == 1, pore_k, solid_k).reshape(slab * length, length)
    along = along.reshape(9, slab * length, 2 * length)
    return along, to_real.T, local_k.T, received


def shards(temperature, choice, location, labels, pair):
    cell_count, macro_count = lax.axis_size("cell"), lax.axis_size("macro")
    slab = labels.shape[1]
    length = slab * cell_count
    devices = macro_count * cell_count
    span = temperature.shape
    rows = span[0] * span[1] * span[2]
    capacity = 2 * rows // devices
    lanes = 128

    tall = neighbours(temperature, "macro", 0)
    wide = neighbours(temperature, "cell", 1)
    deep = jnp.pad(temperature, ((0, 0), (0, 0), (1, 1)))
    gradients = (
        jnp.stack(
            [
                tall[2:] - tall[:-2],
                wide[:, 2:] - wide[:, :-2],
                deep[:, :, 2:] - deep[:, :, :-2],
            ]
        ).reshape(3, rows)
        * 0.5
    )
    units = choice.reshape(rows)
    px, py, pz = location.reshape(3, rows)
    slots = slots_of(units * cell_count + px // slab, devices, capacity)
    offsets = ((px % slab) * length + py) * length + pz
    payload = jnp.concatenate([gradients, offsets.astype(jnp.float32)[None]])
    upper, lower = upper_lower(payload)
    slot_rows = devices * capacity // lanes
    at_row, at_lane = one_hot(slots // lanes, slot_rows), one_hot(slots % lanes, lanes)
    spread = (jnp.stack([upper, lower])[:, :, None, :] * at_row).reshape(8 * slot_rows, rows)
    placed = exact_dot("rn,ln->rl", spread, at_lane).reshape(2, 4, devices, capacity)
    outgoing = (placed[0] + placed[1]).transpose(1, 0, 2)
    received = lax.all_to_all(outgoing, BOTH, split_axis=0, concat_axis=0, tiled=True)
    along, waves, local_k, received = unit_fields(labels, pair, received)
    received = received.transpose(1, 0, 2).reshape(4, devices * capacity)
    got_offset = received[3].astype(jnp.int32)
    found, sums = probe(along, waves, local_k, got_offset // length, got_offset % length)
    found = found.reshape(3, 3, devices * capacity)
    answers = -jnp.sum(found * received[:3, None, :], axis=0)
    answers = answers.reshape(3, devices, capacity).transpose(1, 0, 2)
    shares = jnp.pad(sums[:, 0] / (length * length * length), (0, lanes - 9))
    answers = jnp.concatenate(
        [
            answers.reshape(devices, 3 * capacity),
            jnp.broadcast_to(shares[None, :], (devices, lanes)),
        ],
        axis=1,
    )
    returned = lax.all_to_all(answers, BOTH, split_axis=0, concat_axis=0, tiled=True)
    shares = returned[:, 3 * capacity : 3 * capacity + 9]
    tensors = jnp.sum(shares.reshape(macro_count, cell_count, 9), axis=1).T
    returned = returned[:, : 3 * capacity].reshape(devices, 3, capacity)
    returned = returned.transpose(1, 0, 2).reshape(3, slot_rows, lanes)
    probes = lookup(returned, slots % lanes, slots // lanes)

    marks = (jnp.arange(macro_count)[:, None] == units[None, :]).astype(jnp.float32)
    chosen = jnp.einsum("tu,un->tn", tensors, marks, precision=highest).reshape(3, 3, rows)
    flux = -jnp.sum(chosen * gradients[:, None, :], axis=0)
    return flux.reshape((3,) + span), probes.reshape((3,) + span)


def solution(mesh):
    in_specs = (
        P("macro", "cell", None),
        P("macro", "cell", None),
        P(None, "macro", "cell", None),
        P("macro", "cell", None),
        P("macro", None),
    )
    out_specs = (P(None, "macro", "cell", None), P(None, "macro", "cell", None))
    return jax.shard_map(shards, mesh=mesh, in_specs=in_specs, out_specs=out_specs, check_vma=False)
```

time: 1520 us -> 327 us (0.22)
  local copies, waits for them, and re-layouts: 1090 us -> 25.2 us
  waiting for transfers between devices: 166 us -> 80.9 us
  matrix products: 114 us -> 50.6 us
  Pallas kernels: 0 us -> 56.6 us
  blocking collectives: 25.4 us -> 0 us
    gather x35 -> x0, local copies, waits for them, and re-layouts: 873 us -> none  [the longest x6 272 us: shards(): total = flux_table[0, component][got_offset] * got_grad[0]]
    scatter x2 -> x0, local copies, waits for them, and re-layouts: 139 us -> none  [the longest x1 70.3 us: shards(): jnp.zeros((4, device_count * capacity), jnp.float32).at[:, slot_index]]
    all_to_all x7 -> x4, waiting for transfers between devices: 165 us -> 80.2 us  [the longest x1 35.5 us: unit_fields(): back = lax.all_to_all(back, 'cell', split_axis=2, concat_axis=1, tiled=True)]
    dot_general x20 -> x23, matrix products: 114 us -> 50.6 us  [the longest x19 45.1 us: einsum(): return jnp.einsum(eq, a, b, precision=high)]
    pallas_call x0 -> x2, Pallas kernels: none -> 56.6 us  [the longest x1 50.6 us: probe(): pl.pallas_call(probe_kernel, grid=(count // block,), in_specs=[pl.BlockSp...]
    gather x20 -> x0, other arithmetic: 23.3 us -> none  [the longest x3 22.6 us: shards(): position = jnp.arange(row_count, dtype=jnp.int32) - starts[sorted_targets]]
    all_to_all x9 -> x3, local copies, waits for them, and re-layouts: 24.1 us -> 5.07 us  [the longest x1 3.71 us: unit_fields(): back = lax.all_to_all(back, 'cell', split_axis=2, concat_axis=1, tiled=True)]
    reshape x4 -> x3, local copies, waits for them, and re-layouts: 19.8 us -> 1.23 us  [the longest x1 0.83 us: unit_fields(): sign = jnp.where(whole == 1, 1.0, -1.0).reshape(length, length, length)]
  transfers between devices with their start and end apart: 11 -> 9, of which waited for: 5 -> 3; matrix products, arithmetic and copies ran while one was open for 17% -> 28% of each run, Pallas kernels for 0% -> 0%
where the time goes in v1:
time: 327 us; the launch traced here: 326 us
  waiting for transfers between devices  80.9 us (25%)
  other arithmetic  61.2 us (19%)
  Pallas kernels  56.6 us (17%)
  matrix products  50.6 us (15%)
  starting transfers between devices  33.3 us (10%)
  local copies, waits for them, and re-layouts  25.2 us (8%)
  between operations  17.8 us (5%)
    pallas_call x1, Pallas kernels, probe(): pl.pallas_call(probe_kernel, grid=(count // block,), in_specs=[pl.BlockSp...  50.6 us
    dot_general x19, matrix products, einsum(): return jnp.einsum(eq, a, b, precision=high)  45.1 us
    all_to_all x1, waiting for transfers between devices, unit_fields(): back = lax.all_to_all(back, 'cell', split_axis=2, concat_axis=1, tiled=True)  35.5 us
    all_to_all x1, waiting for transfers between devices, unit_fields(): band = lax.all_to_all(sent, 'cell', split_axis=1, concat_axis=2, tiled=True)  34.9 us
    slice x7, other arithmetic, rotate(): return jnp.concatenate([values[..., half:], -values[..., :half]], axis=-1)  20.5 us
    another operation x2, other arithmetic, unit_fields(): powers = jnp.stack([wx * wx * base, wx * base, base])  16.5 us
    all_to_all x1, starting transfers between devices, shards(): lax.all_to_all(outgoing, BOTH, split_axis=0, concat_axis=0, tiled=True)  9.99 us
    all_to_all x1, waiting for transfers between devices, shards(): lax.all_to_all(answers, BOTH, split_axis=0, concat_axis=0, tiled=True)  9.81 us
  transfers between devices with their start and end apart: 9, of which 3 were waited for; matrix products, arithmetic and copies ran while one was open for 28% of the time, Pallas kernels for 0%

profile of v1, /device:TPU:0, one launch (start us, length us, event | category | flops | bytes accessed | tf_op | source)
XLA Modules:
  0.0 325.6 jit_solution(1930695614728439133)
XLA Ops:
  7.9 1.3 fusion.235
  9.2 2.9 collective-permute-start.1
  12.2 1.3 collective-permute-start
  13.4 1.3 fusion.236
  14.8 4.2 %collective-permute-start.3 = (f32[4,1,128]{2,1,0:T(1,128)}, f32[4,1,128]{2,1,0:T(1,128)S(1)}, u32[]{:S(2)}, u32[]{:S(2)}) collective-permute-start(f32[4,1,128]{2,1,0:T(1,128)} %get-tuple-element.60), channel_id=1, source_target_pairs={{0,1},{1,2},{2,3},{4,5},{5,6},{6,7},{8,9},{9,10},{10,11},{12,13},{... | collective-permute-start | bytes 6152 | tf_op jit(solution)/shard_map/ppermute | solution.py:24
  19.0 1.3 collective-permute-start.2
  20.5 1.3 fusion.237
  25.1 2.3 broadcast_select_fusion
  28.2 0.8 fusion.234
  30.7 1.4 add_select_fusion
  33.7 1.0 fusion.73
  34.9 1.0 mul.614
  36.5 1.1 fusion.100
  38.5 1.4 broadcast_multiply_fusion
  39.9 4.5 %fusion.9 = f32[1024,128]{1,0:T(8,128)S(1)} fusion(bf16[1024,8192]{1,0:T(8,128)(2,1)S(1)} %bitcast.183, s32[8192]{0:T(1024)S(1)} %copy-done.8), kind=kOutput, calls=%fused_computation.22 | convolution fusion | flops 2148532224 | bytes 17334272 | tf_op jit(solution)/shard_map/rn,ln->rl/dot_general | solution.py:181
  44.5 0.9 copy.168
  45.4 10.0 %all-to-all-start = ((f32[32,4,512]{2,1,0:T(4,128)}), f32[32,4,512]{2,1,0:T(4,128)}, u32[]{:S(2)}, u32[]{:S(2)}) async-start(f32[32,4,512]{2,1,0:T(4,128)} %bitcast.171), calls=%async_computation | async-start | bytes 524288 | tf_op jit(solution)/shard_map/all_to_all | solution.py:297
  55.4 1.3 compare_select_fusion
  56.7 0.8 reshape.832
  57.5 1.0 fusion.83
  58.6 1.2 fusion.119
  59.7 0.9 fusion.233
  60.6 1.6 add_bitcast_fusion.2
  62.2 0.9 fusion.232
  63.7 2.3 fusion.49
  66.0 2.8 fusion.44
  69.5 15.7 %pad_maximum_fusion = f32[3,64,64,128]{3,1,2,0:T(8,128)} fusion(f32[1,64,64,128]{3,1,2,0:T(8,128)S(1)} %bitcast.181, f32[1,64,64,128]{3,1,2,0:T(8,128)S(1)} %get-tuple-element.38, f32[1,64,64,128]{3,1,2,0:T(8,128)S(1)} %get-tuple-element.37), kind=kLoop, calls=%fused_computation.3 | loop fusion | flops 3145728 | bytes 12582912 | tf_op jit(solution)/shard_map/stack | solution.py:224
  85.2 1.8 fusion.115
  87.1 11.1 %fusion.226 = (f32[3,64,64,64]{3,1,2,0:T(8,128)}, f32[3,64,64,64]{3,1,2,0:T(8,128)}) fusion(f32[3,64,64,128]{3,1,2,0:T(8,128)} %pad_maximum_fusion), kind=kLoop, calls=%fused_computation.319 | loop fusion | flops 786432 | bytes 12582912 | tf_op jit(solution)/shard_map/slice | solution.py:42
  98.2 6.1 %subtract_bitcast_fusion.1 = f32[3,16,64,128]{3,1,2,0:T(8,128)S(1)} fusion(f32[3,64,128,16]{2,3,1,0:T(8,128)S(1)} %fusion.115, f32[3,64,64,64]{3,1,2,0:T(8,128)} %get-tuple-element.21, f32[3,64,64,64]{3,1,2,0:T(8,128)} %get-tuple-element.20, f32[64,64]{0,1:T(8,128)S(1)} %copy-done.4, s32[]{:T(128)S(6)} %select_n.273), kind=kOutput, calls=%fused_computation.86 | convolution fusion | flops 152961024 | bytes 9453572 | tf_op jit(solution)/shard_map/xk,mkyz->mxyz/dot_general | solution.py:17
  104.9 2.5 fusion.30
  107.4 1.1 fusion.231
  108.5 0.9 pad_maximum_fusion.4
  109.4 2.5 fusion.28
  111.9 1.6 fusion.26
  113.5 1.6 fusion.32
  115.1 1.4 fusion.230
  116.5 2.7 fusion.14
  119.1 1.6 add_bitcast_fusion.1
  122.1 1.7 slice_convert_fusion
  123.8 3.4 %copy.98 = f32[6,64,16,128]{3,2,0,1:T(8,128)} copy(f32[6,64,16,128]{3,1,2,0:T(8,128)S(1)} %pad_maximum_fusion.5) | data formatting | bytes 6291456 | tf_op jit(solution)/shard_map/optimization_barrier | solution.py:245
  127.3 3.9 %all-to-all-start.1 = ((f32[6,64,16,128]{3,2,0,1:T(8,128)}), f32[6,64,16,128]{3,2,0,1:T(8,128)S(1)}, u32[]{:S(2)}, u32[]{:S(2)}) async-start(f32[6,64,16,128]{3,2,0,1:T(8,128)} %copy.98), calls=%async_computation.1 | async-start | bytes 6291456 | tf_op jit(solution)/shard_map/all_to_all | solution.py:246
  131.1 1.7 and_select_fusion
  132.8 34.9 %all-to-all-done.1 = f32[6,64,16,128]{3,2,0,1:T(8,128)S(1)} async-done(((f32[6,64,16,128]{3,2,0,1:T(8,128)}), f32[6,64,16,128]{3,2,0,1:T(8,128)S(1)}, u32[]{:S(2)}, u32[]{:S(2)}) %all-to-all-start.1) | async-done | bytes 3145760 | tf_op jit(solution)/shard_map/all_to_all | solution.py:246
  168.1 1.4 fusion.229
  169.5 2.3 fusion.18
  171.8 1.7 add_bitcast_fusion
  174.0 1.6 fusion.13
  175.6 1.4 fusion.10
  177.0 2.2 subtract_bitcast_fusion
  179.2 3.7 %copy.104 = f32[6,16,64,128]{3,1,0,2:T(8,128)} copy(f32[6,16,64,128]{3,2,1,0:T(8,128)S(1)} %subtract_bitcast_fusion) | data formatting | bytes 6291456 | tf_op jit(solution)/shard_map/sub | solution.py:50
  182.9 4.8 %all-to-all-start.2 = ((f32[6,16,64,128]{3,1,0,2:T(8,128)}), f32[6,16,64,128]{3,1,0,2:T(8,128)}, u32[]{:S(2)}, u32[]{:S(2)}) async-start(f32[6,16,64,128]{3,1,0,2:T(8,128)} %copy.104), calls=%async_computation.2 | async-start | bytes 6291456 | tf_op jit(solution)/shard_map/all_to_all | solution.py:254
  188.0 35.5 %all-to-all-done.2 = f32[6,16,64,128]{3,1,0,2:T(8,128)} async-done(((f32[6,16,64,128]{3,1,0,2:T(8,128)}), f32[6,16,64,128]{3,1,0,2:T(8,128)}, u32[]{:S(2)}, u32[]{:S(2)}) %all-to-all-start.2) | async-done | bytes 3145760 | tf_op jit(solution)/shard_map/all_to_all | solution.py:254
  223.5 3.7 %copy.105 = f32[6,16,64,128]{3,2,1,0:T(8,128)S(1)} copy(f32[6,16,64,128]{3,1,0,2:T(8,128)} %all-to-all-done.2) | data formatting | bytes 6291456 | tf_op jit(solution)/shard_map/all_to_all | solution.py:254
  228.6 1.4 copy.108
  230.0 2.3 fusion.108
  232.4 3.9 %fusion.227 = (f32[9,64,16,64]{3,1,2,0:T(8,128)S(1)}, f32[9,64,16,64]{3,1,2,0:T(8,128)}) fusion(f32[9,64,16,128]{3,1,2,0:T(8,128)S(1)} %bitcast.178), kind=kLoop, calls=%fused_computation.320 | loop fusion | flops 589824 | bytes 9437184 | tf_op jit(solution)/shard_map/slice | solution.py:42
  236.2 5.8 %fusion.37 = f32[9,16,128,64]{2,3,1,0:T(8,128)S(1)} fusion(f32[9,16,128,64]{2,3,1,0:T(8,128)S(1)} %fusion.108, f32[9,64,16,64]{3,1,2,0:T(8,128)} %get-tuple-element.23, f32[9,64,16,64]{3,1,2,0:T(8,128)S(1)} %get-tuple-element.22), kind=kOutput, calls=%fused_computation.60 | convolution fusion | flops 455401472 | bytes 14155776 | tf_op jit(solution)/shard_map/yk,nkxz->nxyz/dot_general | solution.py:17
  242.1 50.6 %shard_map.77 = (f32[9,16384]{1,0:T(8,128)S(1)}, f32[9,128]{1,0:T(8,128)S(1)}) custom-call(s32[1,16384]{1,0:T(1,128)S(1)} %and_select_fusion.1.k_ref, s32[1,16384]{1,0:T(1,128)S(1)} %get-tuple-element.16.l_ref, f32[9,1024,128]{2,1,0:T(8,128)S(1)} %bitcast.174, f32[64,128]{1,0:T(8,128)S(1)} %fusion.149.waves_ref, f32[64,1024]{1,0:T(8,128)S(1)} %bitcast.175), custom_call_target="tpu_custom_call" | custom-call | flops 38654705664 | bytes 4718592 | tf_op jit(solution)/shard_map/pallas_call | solution.py:145
  293.0 1.3 multiply_reduce_fusion
  294.6 0.9 copy.112
  295.5 4.9 %all-to-all-start.3 = ((f32[32,1,1664]{2,1,0:T(1,128)}), f32[32,1,1664]{2,1,0:T(1,128)S(1)}, u32[]{:S(2)}, u32[]{:S(2)}) async-start(f32[32,1,1664]{2,1,0:T(1,128)} %copy.112), calls=%async_computation.3 | async-start | bytes 425984 | tf_op jit(solution)/shard_map/all_to_all | solution.py:313
  300.4 9.8 %all-to-all-done.3 = f32[32,1,1664]{2,1,0:T(1,128)S(1)} async-done(((f32[32,1,1664]{2,1,0:T(1,128)}), f32[32,1,1664]{2,1,0:T(1,128)S(1)}, u32[]{:S(2)}, u32[]{:S(2)}) %all-to-all-start.3) | async-done | bytes 213024 | tf_op jit(solution)/shard_map/all_to_all | solution.py:313
  311.9 6.0 %shard_map.78 = f32[3,8192]{1,0:T(4,128)S(1)} custom-call(s32[1,8192]{1,0:T(1,128)S(1)} %and_select_fusion.3.k_ref, s32[1,8192]{1,0:T(1,128)S(1)} %get-tuple-element.10.l_ref, f32[384,128]{1,0:T(8,128)S(1)} %reshape_reshape.3.table_ref), custom_call_target="tpu_custom_call" | custom-call | flops 1610612736 | bytes 196608 | tf_op jit(solution)/shard_map/pallas_call | solution.py:82
  (111 shorter events, 15.9 us)
Async XLA Ops:
  7.2 48.2 %all-gather.3.cloned.1.call-start = ((), (), s32[]{:S(2)}) async-start(), calls=%async_computation.4 | async-start | bytes 1310720 | tf_op jit(solution)/shard_map/all_gather | solution.py:216
  9.2 27.2 %collective-permute-start.1 = (f32[1,16,128]{2,1,0:T(8,128)}, f32[1,16,128]{2,1,0:T(8,128)}, u32[]{:S(2)}, u32[]{:S(2)}) collective-permute-start(f32[1,16,128]{2,1,0:T(8,128)} %get-tuple-element.58), channel_id=1, source_target_pairs={{0,4},{4,8},{8,12},{12,16},{16,20},{20,24},{24,28},{1,5},{5,9},{9,... | collective-permute-start | bytes 24584 | tf_op jit(solution)/shard_map/ppermute | solution.py:24
  12.2 24.3 %collective-permute-start = (f32[1,16,128]{2,1,0:T(8,128)}, f32[1,16,128]{2,1,0:T(8,128)}, u32[]{:S(2)}, u32[]{:S(2)}) collective-permute-start(f32[1,16,128]{2,1,0:T(8,128)} %get-tuple-element.57), channel_id=1, source_target_pairs={{4,0},{8,4},{12,8},{16,12},{20,16},{24,20},{28,24},{5,1},{9,5},{13... | collective-permute-start | bytes 24584 | tf_op jit(solution)/shard_map/ppermute | solution.py:25
  14.8 21.6 %collective-permute-start.3 = (f32[4,1,128]{2,1,0:T(1,128)}, f32[4,1,128]{2,1,0:T(1,128)S(1)}, u32[]{:S(2)}, u32[]{:S(2)}) collective-permute-start(f32[4,1,128]{2,1,0:T(1,128)} %get-tuple-element.60), channel_id=1, source_target_pairs={{0,1},{1,2},{2,3},{4,5},{5,6},{6,7},{8,9},{9,10},{10,11},{12,13},{... | collective-permute-start | bytes 6152 | tf_op jit(solution)/shard_map/ppermute | solution.py:24
  19.0 17.4 %collective-permute-start.2 = (f32[4,1,128]{2,1,0:T(1,128)}, f32[4,1,128]{2,1,0:T(1,128)}, u32[]{:S(2)}, u32[]{:S(2)}) collective-permute-start(f32[4,1,128]{2,1,0:T(1,128)} %get-tuple-element.59), channel_id=1, source_target_pairs={{1,0},{2,1},{3,2},{5,4},{6,5},{7,6},{9,8},{10,9},{11,10},{13,12},{... | collective-permute-start | bytes 6152 | tf_op jit(solution)/shard_map/ppermute | solution.py:25
  27.5 8.4 %copy-start.10 = (f32[128]{0:T(128)}, f32[128]{0:T(128)S(1)}, u32[]{:S(2)}) copy-start(f32[128]{0:T(128)S(1)} %broadcast_in_dim_tile.15) | copy-start | bytes 1540
  27.5 8.4 %copy-start.13 = (f32[128]{0:T(128)}, f32[128]{0:T(128)S(1)}, u32[]{:S(2)}) copy-start(f32[128]{0:T(128)S(1)} %mul.623) | copy-start | bytes 1540
  38.5 1.4 copy-start.8
  45.4 76.8 %all-to-all-start = ((f32[32,4,512]{2,1,0:T(4,128)}), f32[32,4,512]{2,1,0:T(4,128)}, u32[]{:S(2)}, u32[]{:S(2)}) async-start(f32[32,4,512]{2,1,0:T(4,128)} %bitcast.171), calls=%async_computation | async-start | bytes 524288 | tf_op jit(solution)/shard_map/all_to_all | solution.py:297
  63.7 2.3 copy-start.9
  63.7 2.3 copy-start.14
  87.1 11.1 %copy-start.4 = (f32[64,64]{0,1:T(8,128)S(1)}, f32[64,64]{0,1:T(8,128)}, u32[]{:S(2)}) copy-start(f32[64,64]{0,1:T(8,128)} %fusion.132) | copy-start | bytes 49156
  111.9 1.6 copy-start.1
  111.9 1.6 copy-start.12
  120.8 0.7 copy-start.11
  127.3 40.4 %all-to-all-start.1 = ((f32[6,64,16,128]{3,2,0,1:T(8,128)}), f32[6,64,16,128]{3,2,0,1:T(8,128)S(1)}, u32[]{:S(2)}, u32[]{:S(2)}) async-start(f32[6,64,16,128]{3,2,0,1:T(8,128)} %copy.98), calls=%async_computation.1 | async-start | bytes 6291456 | tf_op jit(solution)/shard_map/all_to_all | solution.py:246
  171.8 1.7 copy-start
  182.9 4.8 %copy-start.2 = (s32[1,32,512]{2,0,1:T(1,128)S(1)}, s32[1,32,512]{2,0,1:T(1,128)}, u32[]{:S(2)}) copy-start(s32[1,32,512]{2,0,1:T(1,128)} %slice_convert_fusion) | copy-start | bytes 196612
  182.9 4.8 %copy-start.3 = (s32[1,16384]{1,0:T(1,128)S(1)}, s32[1,16384]{1,0:T(1,128)}, u32[]{:S(2)}) copy-start(s32[1,16384]{1,0:T(1,128)} %get-tuple-element.17) | copy-start | bytes 196612
  182.9 40.5 %all-to-all-start.2 = ((f32[6,16,64,128]{3,1,0,2:T(8,128)}), f32[6,16,64,128]{3,1,0,2:T(8,128)}, u32[]{:S(2)}, u32[]{:S(2)}) async-start(f32[6,16,64,128]{3,1,0,2:T(8,128)} %copy.104), calls=%async_computation.2 | async-start | bytes 6291456 | tf_op jit(solution)/shard_map/all_to_all | solution.py:254
  292.7 7.7 %copy-start.6 = (s32[1,8192]{1,0:T(1,128)S(1)}, s32[1,8192]{1,0:T(1,128)}, u32[]{:S(2)}) copy-start(s32[1,8192]{1,0:T(1,128)} %get-tuple-element.11) | copy-start | bytes 98308
  292.7 17.8 %copy-start.5 = (s32[4,16,128]{2,1,0:T(8,128)S(1)}, s32[4,16,128]{2,1,0:T(8,128)}, u32[]{:S(2)}) copy-start(s32[4,16,128]{2,1,0:T(8,128)} %param.7) | copy-start | bytes 98308
  292.7 17.8 %copy-start.7 = (f32[3,8192]{1,0:T(4,128)S(1)}, f32[3,8192]{1,0:T(4,128)}, u32[]{:S(2)}) copy-start(f32[3,8192]{1,0:T(4,128)} %get-tuple-element.47) | copy-start | bytes 294916
  295.5 14.8 %all-to-all-start.3 = ((f32[32,1,1664]{2,1,0:T(1,128)}), f32[32,1,1664]{2,1,0:T(1,128)S(1)}, u32[]{:S(2)}, u32[]{:S(2)}) async-start(f32[32,1,1664]{2,1,0:T(1,128)} %copy.112), calls=%async_computation.3 | async-start | bytes 425984 | tf_op jit(solution)/shard_map/all_to_all | solution.py:313
Sparse Core Ops, SparseCore 0:
  9.8 29.3 all-gather.2
